TPU v7x, 32 devices: a whole 2x2x4 slice. The times are simulated.
32 devices in a mesh: sect: 4 (over x, core), dom: 8 (over z, y).
Axes of the slice: x: 2, y: 2, z: 4, core: 2. Of those that a mesh axis runs over, the one named last changes fastest.
Arguments:
- face_sens: bfloat16 [4, 4096, 128], P('sect', 'dom'), may hold values from -6 to 6
- face_owner: int32 [4, 4096], P('sect', 'dom'), may hold values from 0 to 7, as said below
- face_node: int32 [4, 4096], P('sect', 'dom'), may hold values from 0 to 8191
- face_mask: int32 [4, 4096], P('sect', 'dom'), may hold values 0 or 1
- adjoint_prev: bfloat16 [32, 128, 64, 128], P('sect', 'dom'), may hold values from -6 to 6
- block_rows: bfloat16 [32, 128, 64, 384], P('sect', 'dom'), may hold values from -0.3 to 1.7
- coupling: int32 [32, 128, 5], P('sect', 'dom'), may hold values from 0 to 23
Outputs:
- adjoint: bfloat16 [32, 128, 64, 128], P('sect', 'dom')
- face_grad: bfloat16 [4, 4096, 128], P('sect', 'dom')
Inputs may be any that keep to these rules, and one draw needn't show every extreme that they name: `face_owner`: among the 512 faces of one device at most 128 name the same owner; in every passage one owner is named by exactly 128 faces of every device.
All inputs are finite; a program needn't handle non-finite values. No bound on the sum of `face_mask` on one device may be relied on, other than what follows from the above.
Results may differ from a plain program's by a relative error of at most 0.0062.
Values may be sent and summed in bfloat16 or wider, within the bound.
A program may use at most 128 MiB of HBM per device.

v0:
```python
import jax
import jax.numpy as jnp
from jax import lax
from jax.sharding import PartitionSpec as P

SWEEPS = 2


def with_halo(block, sides, width, periodic):
    for axis, dim in sides:
        count = lax.axis_size(axis)
        forward = [(i, i + 1) for i in range(count - 1)]
        if periodic:
            forward.append((count - 1, 0))
        backward = [(target, source) for source, target in forward]
        low = lax.ppermute(
            lax.slice_in_dim(block, block.shape[dim] - width, None, axis=dim), axis, forward
        )
        high = lax.ppermute(lax.slice_in_dim(block, 0, width, axis=dim), axis, backward)
        block = jnp.concatenate([low, block, high], axis=dim)
    return block


def place_code(code_value):
    position = code_value + (code_value >= 12).astype(jnp.int32)
    return (position // 5 - 2, position % 5 - 2)


def load_nodes(slot_rows, slot_nodes, circ_blocks, span):
    local = jnp.arange(span, dtype=jnp.int32)

    def one_block(circ_row):
        hit = (slot_nodes[None, :] - circ_row * span == local[:, None]).astype(jnp.bfloat16)
        return jnp.dot(hit, slot_rows, preferred_element_type=jnp.float32)

    return lax.map(one_block, jnp.arange(circ_blocks, dtype=jnp.int32))


def pick_nodes(flat_adjoint, slot_nodes, span):
    local = jnp.arange(span, dtype=jnp.int32)
    start = jnp.zeros((slot_nodes.shape[0], flat_adjoint.shape[2]), jnp.float32)

    def add_block(total, inputs):
        circ_row, block = inputs
        hit = (slot_nodes[:, None] - circ_row * span == local[None, :]).astype(jnp.bfloat16)
        return (total + jnp.dot(hit, block, preferred_element_type=jnp.float32), None)

    circ_ids = jnp.arange(flat_adjoint.shape[0], dtype=jnp.int32)
    total, unused = lax.scan(add_block, start, (circ_ids, flat_adjoint))
    return total.astype(jnp.bfloat16)


def shards(face_sens, face_owner, face_node, face_mask, adjoint_prev, block_rows, coupling):
    peer_count = lax.axis_size("dom")
    my_index = lax.axis_index("dom")
    face_count = face_sens.shape[1]
    columns = face_sens.shape[2]
    circ_blocks = adjoint_prev.shape[0]
    radial_blocks = adjoint_prev.shape[1]
    tile_size = adjoint_prev.shape[2]
    coupled_count = coupling.shape[2]
    span = radial_blocks * tile_size
    per_peer = 2 * face_count // peer_count
    owner_ids = face_owner[0]
    node_ids = face_node[0]
    live_factor = face_mask[0].astype(jnp.bfloat16)[:, None]
    face_rows = face_sens[0] * live_factor
    peer_ids = jnp.arange(peer_count, dtype=jnp.int32)
    slot_ids = jnp.arange(per_peer, dtype=jnp.int32)
    owner_table = (owner_ids[None, :] == peer_ids[:, None]).astype(jnp.int32)
    rank_index = jnp.sum(owner_table * (jnp.cumsum(owner_table, axis=1) - 1), axis=0)
    send_hit = (owner_table[:, None, :] > 0) & (
        rank_index[None, None, :] == slot_ids[None, :, None]
    )
    send_weight = send_hit.astype(jnp.bfloat16)
    all_rows, all_owners, all_nodes = (
        lax.all_gather(face_rows, "dom", axis=0, tiled=True),
        lax.all_gather(owner_ids, "dom", axis=0, tiled=True),
        lax.all_gather(node_ids, "dom", axis=0, tiled=True),
    )
    mine_table = (all_owners == my_index).reshape(peer_count, face_count).astype(jnp.int32)
    mine_rank = jnp.cumsum(mine_table, axis=1) - 1
    got_hit = (mine_table[:, None, :] > 0) & (mine_rank[:, None, :] == slot_ids[None, :, None])
    source_rows = all_rows.reshape(peer_count, face_count, columns)
    got_rows = jnp.einsum(
        "jsf,jfc->jsc",
        got_hit.astype(jnp.bfloat16),
        source_rows,
        preferred_element_type=jnp.float32,
    ).astype(jnp.bfloat16)
    got_nodes = jnp.sum(
        got_hit.astype(jnp.int32) * all_nodes.reshape(peer_count, 1, face_count), axis=2
    )
    slot_nodes = got_nodes.reshape(-1)
    node_load = load_nodes(got_rows.reshape(-1, columns), slot_nodes, circ_blocks, span)
    node_load = node_load.reshape(circ_blocks, radial_blocks, tile_size, columns)
    shift_circ, shift_radial = place_code(coupling)
    pick_circ = jnp.arange(circ_blocks, dtype=jnp.int32)[:, None, None] + 2 + shift_circ
    pick_radial = jnp.arange(radial_blocks, dtype=jnp.int32)[None, :, None] + 2 + shift_radial
    pick_index = (pick_circ * (radial_blocks + 4) + pick_radial).reshape(-1)
    inverse = block_rows[:, :, :, :tile_size]
    coupled_tiles = block_rows[:, :, :, tile_size:]
    iterate = adjoint_prev
    for sweep_index in range(SWEEPS):
        circ_padded = with_halo(iterate, (("sect", 0),), 2, True)
        padded = with_halo(circ_padded, (("dom", 1),), 2, False)
        flat_blocks = padded.reshape(-1, tile_size, columns)
        neighbours = jnp.take(flat_blocks, pick_index, axis=0).reshape(
            circ_blocks, radial_blocks, coupled_count * tile_size, columns
        )
        coupled = jnp.einsum(
            "cbij,cbjd->cbid", coupled_tiles, neighbours, preferred_element_type=jnp.float32
        )
        remainder = (node_load - coupled).astype(jnp.bfloat16)
        iterate = jnp.einsum(
            "cbij,cbjd->cbid", inverse, remainder, preferred_element_type=jnp.float32
        ).astype(jnp.bfloat16)
    reply_rows = pick_nodes(iterate.reshape(circ_blocks, span, columns), slot_nodes, span).reshape(
        peer_count, per_peer, columns
    )
    returned = lax.all_to_all(reply_rows, "dom", split_axis=0, concat_axis=0, tiled=True)
    face_rows_back = jnp.einsum(
        "jsf,jsc->fc", send_weight, returned, preferred_element_type=jnp.float32
    ).astype(jnp.bfloat16)
    face_grad = face_rows_back * live_factor
    return (iterate, face_grad[None])


def solution(mesh):
    placed = (
        P("sect", "dom", None),
        P("sect", "dom"),
        P("sect", "dom"),
        P("sect", "dom"),
        P("sect", "dom", None, None),
        P("sect", "dom", None, None),
        P("sect", "dom", None),
    )
    return jax.shard_map(
        shards,
        mesh=mesh,
        in_specs=placed,
        out_specs=(P("sect", "dom", None, None), P("sect", "dom", None)),
        check_vma=False,
    )
```

profile of v0, /device:TPU:1, one launch (start us, length us, event | category | flops | bytes accessed | tf_op | source)
XLA Modules:
  0.0 277.6 jit_solution(482512775271472238)
XLA Ops:
  8.7 1.7 bitcast_multiply_fusion
  10.4 2.3 fusion.64
  12.6 2.6 collective-permute-start
  15.2 22.0 %all-gather = s32[1,4096]{1,0:T(1,128)S(1)} all-gather(s32[1,512]{1,0:T(1,128)} %param.14), channel_id=2, replica_groups=mesh['sect'=4,'dom'=8] {'dom'}, dimensions={1}, use_global_device_ids=true | all-gather | bytes 18432 | tf_op jit(solution)/shard_map/all_gather | solution.py:78
  40.0 21.9 %all-gather.1 = s32[1,4096]{1,0:T(1,128)S(1)} all-gather(s32[1,512]{1,0:T(1,128)} %param.15), channel_id=3, replica_groups=mesh['sect'=4,'dom'=8] {'dom'}, dimensions={1}, use_global_device_ids=true | all-gather | bytes 18432 | tf_op jit(solution)/shard_map/all_gather | solution.py:79
  63.9 2.2 collective-permute-start.2
  67.9 7.1 %collective-permute-done.2 = bf16[12,2,64,128]{3,2,1,0:T(8,128)(2,1)S(1)} collective-permute-done((bf16[12,2,64,128]{3,2,1,0:T(8,128)(2,1)S(1)}, bf16[12,2,64,128]{3,2,1,0:T(8,128)(2,1)S(1)}, u32[]{:S(2)}, u32[]{:S(2)}) %collective-permute-start.2) | collective-permute-done | bytes 393248 | tf_op jit(solution)/shard_map/ppermute | solution.py:16
  75.0 2.1 pad_maximum_fusion
  77.2 21.8 %gather_fusion = bf16[640,64,128]{2,1,0:T(8,128)(2,1)} fusion(bf16[240,64,128]{2,1,0:T(8,128)(2,1)} %bitcast.76, s32[1024]{0:T(1024)S(1)} %pad_clamp_fusion), kind=kCustom, calls=%fused_computation.clone | custom fusion | bytes 20974080 | tf_op jit(solution)/shard_map/jit(_take)/gather | solution.py:108
  98.9 10.8 %broadcast_select_fusion = bf16[640,64,128]{2,1,0:T(8,128)(2,1)} fusion(bf16[640,64,128]{2,1,0:T(8,128)(2,1)} %gather_fusion, pred[640]{0:T(1024)(128)(4,1)S(1)} %compare_and_fusion), kind=kLoop, calls=%fused_computation.18 | loop fusion | flops 5242880 | bytes 20972160 | tf_op jit(solution)/shard_map/jit(_take)/select_n | solution.py:108
  109.7 1.8 fusion.35
  111.5 22.7 %while.22 = (s32[]{:T(128)}, f32[8,1024,128]{2,1,0:T(8,128)}, s32[8]{0:T(128)S(1)}, s32[8,128]{1,0:T(8,128)S(1)}, bf16[1024,128]{1,0:T(8,128)(2,1)S(1)}, /*index=5*/s32[]{:T(128)}, s32[1]{0:T(128)}) while((s32[]{:T(128)}, f32[8,1024,128]{2,1,0:T(8,128)}, s32[8]{0:T(128)S(1)}, s32[8,128]{1,0:T(8,128)S(1)}, ...), condition=%wide.region_4.5_spmd.clone, body=%wide.region_3.4_spmd.clone.sunk | while | flops 269485056 | bytes 799337 | solution.py:36
  112.8 1.6 fusion.75
  115.6 1.6 fusion.75
  121.3 1.6 fusion.75
  124.1 1.6 fusion.75
  127.0 1.6 fusion.75
  132.7 1.6 fusion.75
  134.3 10.4 %convert_bitcast_fusion = bf16[8,16,64,128]{3,2,1,0:T(8,128)(2,1)S(1)} fusion(bf16[8,16,64,384]{3,2,1,0:T(8,128)(2,1)} %param.18, f32[8,16,64,128]{3,2,1,0:T(8,128)} %bitcast.79, bf16[8,16,320,128]{3,2,1,0:T(8,128)(2,1)} %bitcast.77), kind=kOutput, calls=%fused_computation.30 | convolution fusion | flops 808452096 | bytes 25165824 | tf_op jit(solution)/shard_map/cbij,cbjd->cbid/dot_general | solution.py:115
  144.7 10.9 %collective-permute-start.4 = (bf16[2,16,64,128]{3,2,1,0:T(8,128)(2,1)S(1)}, bf16[2,16,64,128]{3,2,1,0:T(8,128)(2,1)S(1)}, u32[]{:S(2)}, u32[]{:S(2)}) collective-permute-start(bf16[2,16,64,128]{3,2,1,0:T(8,128)(2,1)S(1)} %get-tuple-element.127), channel_id=1, source_target_pairs={{0,8},{8,16},{16,24},{24,0},{1,9},{9,17},{17,25},{25,1},{2,10},{10... | collective-permute-start | bytes 1572872 | tf_op jit(solution)/shard_map/ppermute | solution.py:16
  155.7 11.0 %collective-permute-done.4 = bf16[2,16,64,128]{3,2,1,0:T(8,128)(2,1)S(1)} collective-permute-done((bf16[2,16,64,128]{3,2,1,0:T(8,128)(2,1)S(1)}, bf16[2,16,64,128]{3,2,1,0:T(8,128)(2,1)S(1)}, u32[]{:S(2)}, u32[]{:S(2)}) %collective-permute-start.4) | collective-permute-done | bytes 524320 | tf_op jit(solution)/shard_map/ppermute | solution.py:16
  169.0 4.5 %collective-permute-start.6 = (bf16[12,2,64,128]{3,2,1,0:T(8,128)(2,1)}, bf16[12,2,64,128]{3,2,1,0:T(8,128)(2,1)S(1)}, u32[]{:S(2)}, u32[]{:S(2)}) collective-permute-start(bf16[12,2,64,128]{3,2,1,0:T(8,128)(2,1)} %get-tuple-element.123), channel_id=1, source_target_pairs={{0,1},{1,2},{2,3},{3,4},{4,5},{5,6},{6,7},{8,9},{9,10},{10,11},{11... | collective-permute-start | bytes 1179656 | tf_op jit(solution)/shard_map/ppermute | solution.py:16
  175.5 3.1 %reduce-window.16 = s32[8,4,128]{2,0,1:T(8,128)} reduce-window(s32[8,4,128]{2,0,1:T(8,128)} %fusion.61, s32[]{:T(128)} %constant.69.clone.1), window={size=1x1x128 pad=0_0x0_0x127_0}, to_apply=%region_5.7 | reduce-window | flops 520192 | bytes 32772 | tf_op jit(solution)/shard_map/reduce-window.2
  180.8 10.1 %collective-permute-done.6 = bf16[12,2,64,128]{3,2,1,0:T(8,128)(2,1)S(1)} collective-permute-done((bf16[12,2,64,128]{3,2,1,0:T(8,128)(2,1)}, bf16[12,2,64,128]{3,2,1,0:T(8,128)(2,1)S(1)}, u32[]{:S(2)}, u32[]{:S(2)}) %collective-permute-start.6) | collective-permute-done | bytes 393248 | tf_op jit(solution)/shard_map/ppermute | solution.py:16
  190.9 3.2 %pad_maximum_fusion.1 = bf16[12,20,64,128]{3,2,1,0:T(8,128)(2,1)} fusion(bf16[12,2,64,128]{3,2,1,0:T(8,128)(2,1)} %collective-permute-done.7, bf16[2,16,64,128]{3,2,1,0:T(8,128)(2,1)S(1)} %collective-permute-done.5, bf16[8,16,64,128]{3,2,1,0:T(8,128)(2,1)S(1)} %convert_bitcast_fusion, bf16[2,16,64,128]{3,2,1,0:T(8,128)(2,1)S(1)} %collective-permute-done.4, ...), kind=kLoop, calls=%fused_computation.29 | loop fusion | flops 7864320 | bytes 7864320 | tf_op jit(solution)/shard_map/concatenate | solution.py:20
  194.1 21.8 %gather_fusion.1 = bf16[640,64,128]{2,1,0:T(8,128)(2,1)} fusion(bf16[240,64,128]{2,1,0:T(8,128)(2,1)} %bitcast.75, s32[1024]{0:T(1024)S(1)} %pad_clamp_fusion), kind=kCustom, calls=%fused_computation.1.clone | custom fusion | bytes 20974080 | tf_op jit(solution)/shard_map/jit(_take)/gather | solution.py:108
  215.9 10.8 %broadcast_select_fusion.1 = bf16[640,64,128]{2,1,0:T(8,128)(2,1)} fusion(bf16[640,64,128]{2,1,0:T(8,128)(2,1)} %gather_fusion.1, pred[640]{0:T(1024)(128)(4,1)S(1)} %copy-done.7), kind=kLoop, calls=%fused_computation.19 | loop fusion | flops 5242880 | bytes 20972160 | tf_op jit(solution)/shard_map/jit(_take)/select_n | solution.py:108
  226.7 10.4 %convolution_convert_fusion = bf16[8,16,128,64]{2,3,1,0:T(8,128)(2,1)S(1)} fusion(bf16[8,16,64,384]{3,2,1,0:T(8,128)(2,1)} %param.18, f32[8,16,64,128]{3,2,1,0:T(8,128)} %bitcast.80, bf16[8,16,320,128]{3,2,1,0:T(8,128)(2,1)} %bitcast.78), kind=kOutput, calls=%fused_computation.37 | convolution fusion | flops 808452096 | bytes 25165824 | tf_op jit(solution)/shard_map/cbij,cbjd->cbid/dot_general | solution.py:115
  237.2 18.1 %while.23 = (s32[]{:T(128)}, f32[1024,128]{1,0:T(8,128)S(1)}, s32[8]{0:T(128)S(1)}, s32[8,128]{1,0:T(8,128)S(1)}, bf16[8,1024,128]{2,1,0:T(8,128)(2,1)S(1)}, /*index=5*/s32[]{:T(128)}, s32[1]{0:T(128)}, s32[]{:T(128)}) while((s32[]{:T(128)}, f32[1024,128]{1,0:T(8,128)S(1)}, s32[8]{0:T(128)S(1)}, s32[8,128]{1,0:T(8,128)S(1)}, ...), condition=%wide.region_9.11_spmd.clone, body=%wide.region_8.10_spmd.clone.sunk | while | flops 269747200 | bytes 1323135 | solution.py:49
  256.1 5.4 %all-to-all-start = ((bf16[8,128,128]{2,1,0:T(8,128)(2,1)}), bf16[8,128,128]{2,1,0:T(8,128)(2,1)S(1)}, u32[]{:S(2)}, u32[]{:S(2)}) async-start(bf16[8,128,128]{2,1,0:T(8,128)(2,1)} %bitcast.18), calls=%async_computation | async-start | bytes 524288 | tf_op jit(solution)/shard_map/all_to_all | solution.py:121
  261.8 7.4 %all-to-all-done = bf16[8,128,128]{2,1,0:T(8,128)(2,1)S(1)} async-done(((bf16[8,128,128]{2,1,0:T(8,128)(2,1)}), bf16[8,128,128]{2,1,0:T(8,128)(2,1)S(1)}, u32[]{:S(2)}, u32[]{:S(2)}) %all-to-all-start) | async-done | bytes 262176 | tf_op jit(solution)/shard_map/all_to_all | solution.py:121
  269.2 1.6 fusion.47
  (114 shorter events, 35.9 us)
Async XLA Ops:
  7.2 56.1 %copy-start = (bf16[8,16,64,128]{3,2,1,0:T(8,128)(2,1)S(1)}, bf16[8,16,64,128]{3,2,1,0:T(8,128)(2,1)}, u32[]{:S(2)}) copy-start(bf16[8,16,64,128]{3,2,1,0:T(8,128)(2,1)} %param.17) | copy-start | bytes 6291460
  7.2 102.5 %all-gather.4.cloned.1.call-start = ((), (), s32[]{:S(2)}) async-start(), calls=%async_computation.1 | async-start | bytes 1179648 | tf_op jit(solution)/shard_map/all_gather | solution.py:77
  8.1 0.6 copy-start.8
  12.6 50.6 %collective-permute-start = (bf16[2,16,64,128]{3,2,1,0:T(8,128)(2,1)}, bf16[2,16,64,128]{3,2,1,0:T(8,128)(2,1)S(1)}, u32[]{:S(2)}, u32[]{:S(2)}) collective-permute-start(bf16[2,16,64,128]{3,2,1,0:T(8,128)(2,1)} %get-tuple-element.130), channel_id=1, source_target_pairs={{0,8},{8,16},{16,24},{24,0},{1,9},{9,17},{17,25},{25,1},{2,10},{10... | collective-permute-start | bytes 1572872 | tf_op jit(solution)/shard_map/ppermute | solution.py:16
  15.2 48.5 %collective-permute-start.1 = (bf16[2,16,64,128]{3,2,1,0:T(8,128)(2,1)}, bf16[2,16,64,128]{3,2,1,0:T(8,128)(2,1)S(1)}, u32[]{:S(2)}, u32[]{:S(2)}) collective-permute-start(bf16[2,16,64,128]{3,2,1,0:T(8,128)(2,1)} %get-tuple-element.129), channel_id=1, source_target_pairs={{8,0},{16,8},{24,16},{0,24},{9,1},{17,9},{25,17},{1,25},{10,2},{18... | collective-permute-start | bytes 1572872 | tf_op jit(solution)/shard_map/ppermute | solution.py:19
  63.9 11.1 %collective-permute-start.2 = (bf16[12,2,64,128]{3,2,1,0:T(8,128)(2,1)S(1)}, bf16[12,2,64,128]{3,2,1,0:T(8,128)(2,1)S(1)}, u32[]{:S(2)}, u32[]{:S(2)}) collective-permute-start(bf16[12,2,64,128]{3,2,1,0:T(8,128)(2,1)S(1)} %get-tuple-element.125), channel_id=1, source_target_pairs={{0,1},{1,2},{2,3},{3,4},{4,5},{5,6},{6,7},{8,9},{9,10},{10,11},{11... | collective-permute-start | bytes 1179656 | tf_op jit(solution)/shard_map/ppermute | solution.py:16
  66.1 8.9 %collective-permute-start.3 = (bf16[12,2,64,128]{3,2,1,0:T(8,128)(2,1)S(1)}, bf16[12,2,64,128]{3,2,1,0:T(8,128)(2,1)S(1)}, u32[]{:S(2)}, u32[]{:S(2)}) collective-permute-start(bf16[12,2,64,128]{3,2,1,0:T(8,128)(2,1)S(1)} %get-tuple-element.126), channel_id=1, source_target_pairs={{1,0},{2,1},{3,2},{4,3},{5,4},{6,5},{7,6},{9,8},{10,9},{11,10},{12... | collective-permute-start | bytes 1179656 | tf_op jit(solution)/shard_map/ppermute | solution.py:19
  67.9 31.0 %copy-start.6 = (pred[640]{0:T(1024)(128)(4,1)}, pred[640]{0:T(1024)(128)(4,1)S(1)}, u32[]{:S(2)}) copy-start(pred[640]{0:T(1024)(128)(4,1)S(1)} %compare_and_fusion) | copy-start | bytes 1924
  144.6 30.2 %copy-start.4 = (s32[1,512]{1,0:T(1,128)S(1)}, s32[1,512]{1,0:T(1,128)}, u32[]{:S(2)}) copy-start(s32[1,512]{1,0:T(1,128)} %param.14) | copy-start | bytes 6148
  144.7 22.0 %collective-permute-start.4 = (bf16[2,16,64,128]{3,2,1,0:T(8,128)(2,1)S(1)}, bf16[2,16,64,128]{3,2,1,0:T(8,128)(2,1)S(1)}, u32[]{:S(2)}, u32[]{:S(2)}) collective-permute-start(bf16[2,16,64,128]{3,2,1,0:T(8,128)(2,1)S(1)} %get-tuple-element.127), channel_id=1, source_target_pairs={{0,8},{8,16},{16,24},{24,0},{1,9},{9,17},{17,25},{25,1},{2,10},{10... | collective-permute-start | bytes 1572872 | tf_op jit(solution)/shard_map/ppermute | solution.py:16
  155.7 12.3 %collective-permute-start.5 = (bf16[2,16,64,128]{3,2,1,0:T(8,128)(2,1)S(1)}, bf16[2,16,64,128]{3,2,1,0:T(8,128)(2,1)S(1)}, u32[]{:S(2)}, u32[]{:S(2)}) collective-permute-start(bf16[2,16,64,128]{3,2,1,0:T(8,128)(2,1)S(1)} %get-tuple-element.128), channel_id=1, source_target_pairs={{8,0},{16,8},{24,16},{0,24},{9,1},{17,9},{25,17},{1,25},{10,2},{18... | collective-permute-start | bytes 1572872 | tf_op jit(solution)/shard_map/ppermute | solution.py:19
  169.0 21.9 %collective-permute-start.6 = (bf16[12,2,64,128]{3,2,1,0:T(8,128)(2,1)}, bf16[12,2,64,128]{3,2,1,0:T(8,128)(2,1)S(1)}, u32[]{:S(2)}, u32[]{:S(2)}) collective-permute-start(bf16[12,2,64,128]{3,2,1,0:T(8,128)(2,1)} %get-tuple-element.123), channel_id=1, source_target_pairs={{0,1},{1,2},{2,3},{3,4},{4,5},{5,6},{6,7},{8,9},{9,10},{10,11},{11... | collective-permute-start | bytes 1179656 | tf_op jit(solution)/shard_map/ppermute | solution.py:16
  173.5 17.4 %collective-permute-start.7 = (bf16[12,2,64,128]{3,2,1,0:T(8,128)(2,1)}, bf16[12,2,64,128]{3,2,1,0:T(8,128)(2,1)}, u32[]{:S(2)}, u32[]{:S(2)}) collective-permute-start(bf16[12,2,64,128]{3,2,1,0:T(8,128)(2,1)} %get-tuple-element.124), channel_id=1, source_target_pairs={{1,0},{2,1},{3,2},{4,3},{5,4},{6,5},{7,6},{9,8},{10,9},{11,10},{12... | collective-permute-start | bytes 1179656 | tf_op jit(solution)/shard_map/ppermute | solution.py:19
  180.8 35.1 %copy-start.5 = (s32[8,5]{0,1:T(8,128)}, s32[8,5]{0,1:T(8,128)S(1)}, u32[]{:S(2)}) copy-start(s32[8,5]{0,1:T(8,128)S(1)} %reduce-window.19) | copy-start | bytes 484
  194.1 21.8 %copy-start.7 = (pred[640]{0:T(1024)(128)(4,1)S(1)}, pred[640]{0:T(1024)(128)(4,1)}, u32[]{:S(2)}) copy-start(pred[640]{0:T(1024)(128)(4,1)} %copy-done.6) | copy-start | bytes 1924
  226.7 10.4 %copy-start.2 = (f32[1024,128]{1,0:T(8,128)S(1)}, f32[1024,128]{1,0:T(8,128)}, u32[]{:S(2)}) copy-start(f32[1024,128]{1,0:T(8,128)} %custom-call) | copy-start | bytes 1572868
  237.2 24.4 %copy-start.3 = (s32[8,4,128]{2,0,1:T(8,128)S(1)}, s32[8,4,128]{2,0,1:T(8,128)}, u32[]{:S(2)}) copy-start(s32[8,4,128]{2,0,1:T(8,128)} %reduce-window.16) | copy-start | bytes 49156
  237.2 24.4 %slice-start = ((s32[8,5]{0,1:T(8,128)}), s32[8,4]{0,1:T(4,128)S(1)}, s32[]{:S(2)}) async-start(s32[8,5]{0,1:T(8,128)} %copy-done.5), calls=%async_computation.2 | async-start | bytes 4096 | tf_op jit(solution)/shard_map/slice.3
  237.2 32.0 %copy-start.9 = (bf16[512]{0:T(512)(128)(2,1)S(1)}, bf16[512]{0:T(512)(128)(2,1)}, u32[]{:S(2)}) copy-start(bf16[512]{0:T(512)(128)(2,1)} %copy-done.8) | copy-start | bytes 3076
  255.3 15.5 %copy-start.1 = (bf16[8,1024,128]{2,1,0:T(8,128)(2,1)}, bf16[8,1024,128]{2,1,0:T(8,128)(2,1)S(1)}, u32[]{:S(2)}) copy-start(bf16[8,1024,128]{2,1,0:T(8,128)(2,1)S(1)} %get-tuple-element.239) | copy-start | bytes 6291460
  256.1 13.1 %all-to-all-start = ((bf16[8,128,128]{2,1,0:T(8,128)(2,1)}), bf16[8,128,128]{2,1,0:T(8,128)(2,1)S(1)}, u32[]{:S(2)}, u32[]{:S(2)}) async-start(bf16[8,128,128]{2,1,0:T(8,128)(2,1)} %bitcast.18), calls=%async_computation | async-start | bytes 524288 | tf_op jit(solution)/shard_map/all_to_all | solution.py:121
Sparse Core Ops, SparseCore 0:
  10.7 41.3 all-gather.3
where the time goes:
time: 281 us; the launch traced here: 278 us
  local copies, waits for them, and re-layouts  59.1 us (21%)
  matrix products  44.8 us (16%)
  blocking collectives  44 us (16%)
  other arithmetic  39.3 us (14%)
  waiting for transfers between devices  37 us (13%)
  starting transfers between devices  28.4 us (10%)
  between operations  14.4 us (5%)
  loops' own time  10.8 us (4%)
    gather x2, local copies, waits for them, and re-layouts, shards(): jnp.take(flat_blocks, pick_index, axis=0)  43.5 us
    ppermute x4, waiting for transfers between devices, with_halo(): lax.ppermute(lax.slice_in_dim(block, block.shape[dim] - width, None, axis...  28.2 us
    all_gather x1, blocking collectives, shards(): lax.all_gather(owner_ids, 'dom', axis=0, tiled=True)  22 us
    all_gather x1, blocking collectives, shards(): lax.all_gather(node_ids, 'dom', axis=0, tiled=True)  21.9 us
    select_n x3, other arithmetic, shards(): jnp.take(flat_blocks, pick_index, axis=0)  21.5 us
    dot_general x2, matrix products, shards(): jnp.einsum('cbij,cbjd->cbid', inverse, remainder, preferred_element_type=...  20.8 us
    ppermute x4, starting transfers between devices, with_halo(): lax.ppermute(lax.slice_in_dim(block, block.shape[dim] - width, None, axis...  20.3 us
    dot_general x8, matrix products, one_block(): return jnp.dot(hit, slot_rows, preferred_element_type=jnp.float32)  12.8 us
  transfers between devices with their start and end apart: 10, of which 5 were waited for; matrix products, arithmetic and copies ran while one was open for 17% of the time, Pallas kernels for 0%

commit v1 on v0

v1 whole, which is shorter than its diff:
```python
import functools

import jax
import jax.numpy as jnp
from jax import lax
from jax.experimental import pallas as pl
from jax.experimental.pallas import tpu as pltpu
from jax.sharding import PartitionSpec as P

MESH = pl.DeviceIdType.MESH
F32 = jnp.float32
BF16 = jnp.bfloat16


def kernel(
    sect_n, dom_n, per_peer,
    sens_ref, owner_ref, node_ref, mask_ref, coupling_ref, adj_ref, block_ref,
    adj_out, grad_out,
    pad0, pad1, tiles, load, final, result, weight,
    rows_send, rows_recv, ids_send, ids_recv, reply_f32, reply_send, reply_recv,
    ids_smem, pick_c, pick_r,
    halo_send, halo_recv, face_send, face_recv, id_send, id_recv, back_send, back_recv,
    local_sem, out_sem,
):
    circ, radial, tile, cols = adj_ref.shape
    codes = coupling_ref.shape[2]
    faces = sens_ref.shape[1]
    span = radial * tile
    slots = dom_n * per_peer
    s = lax.axis_index("sect")
    d = lax.axis_index("dom")
    left = lax.rem(s + sect_n - 1, sect_n)
    right = lax.rem(s + 1, sect_n)
    has_lo = d > 0
    has_hi = d < dom_n - 1

    copy_adj = pltpu.make_async_copy(
        adj_ref, pad0.at[2:circ + 2, 2:radial + 2], local_sem.at[0]
    )
    copy_tiles = pltpu.make_async_copy(block_ref, tiles, local_sem.at[1])
    copy_adj.start()
    copy_tiles.start()

    barrier = pltpu.get_barrier_semaphore()
    for side in (left, right):
        pl.semaphore_signal(barrier, inc=1, device_id={"sect": side}, device_id_type=MESH)
    for k in range(1, dom_n):
        pl.semaphore_signal(
            barrier, inc=1, device_id={"dom": lax.rem(d + k, dom_n)}, device_id_type=MESH
        )

    owner = owner_ref[...]
    peers = max(dom_n, 8)
    hot = lax.broadcasted_iota(jnp.int32, (peers, faces), 0) == owner
    hot_f = hot.astype(F32)
    before = lax.broadcasted_iota(jnp.int32, (faces, faces), 0)
    upto = before <= lax.broadcasted_iota(jnp.int32, (faces, faces), 1)
    count = jnp.dot(
        hot_f.astype(BF16), upto.astype(F32).astype(BF16), preferred_element_type=F32
    )
    rank = jnp.sum(hot_f * (count - 1.0), axis=0, keepdims=True).astype(jnp.int32)
    slot = jnp.where(mask_ref[...] > 0, owner * per_peer + rank, -1)
    node = node_ref[...]
    node_hi = jnp.broadcast_to((node // 64).astype(F32), (8, faces)).astype(BF16)
    node_lo = jnp.broadcast_to((node % 64).astype(F32), (8, faces)).astype(BF16)
    weight[...] = (
        (lax.broadcasted_iota(jnp.int32, (slots, faces), 0) == slot).astype(F32).astype(BF16)
    )
    rows_send[...] = jnp.dot(
        weight[...], sens_ref[0], preferred_element_type=F32
    ).astype(BF16)
    across = (((1,), (1,)), ((), ()))
    for j in range(dom_n):
        if per_peer == 128:
            chosen = weight[j * per_peer:(j + 1) * per_peer, :]
        else:
            place = lax.broadcasted_iota(jnp.int32, (128, faces), 0)
            place = place - lax.rem(d * per_peer, 128)
            inside = (place >= 0) & (place < per_peer) & (place + j * per_peer == slot)
            chosen = inside.astype(F32).astype(BF16)
        high = lax.dot_general(node_hi, chosen, across, preferred_element_type=F32)
        low = lax.dot_general(node_lo, chosen, across, preferred_element_type=F32)
        ids_send[j] = (high * 64.0 + low).astype(jnp.int32)

    pl.semaphore_wait(barrier, dom_n + 1)

    def part(start):
        return pl.ds(pl.multiple_of(start * per_peer, per_peer), per_peer)

    def face_copies(k):
        j = lax.rem(d + k, dom_n)
        ids = pltpu.make_async_remote_copy(
            src_ref=ids_send.at[j], dst_ref=ids_recv.at[d],
            send_sem=id_send.at[k], recv_sem=id_recv.at[k],
            device_id={"dom": j}, device_id_type=MESH,
        )
        rows = pltpu.make_async_remote_copy(
            src_ref=rows_send.at[part(j)], dst_ref=rows_recv.at[part(d)],
            send_sem=face_send.at[k], recv_sem=face_recv.at[k],
            device_id={"dom": j}, device_id_type=MESH,
        )
        return ids, rows

    def back_copy(k):
        j = lax.rem(d + k, dom_n)
        return pltpu.make_async_remote_copy(
            src_ref=reply_send.at[part(j)], dst_ref=reply_recv.at[part(d)],
            send_sem=back_send.at[k], recv_sem=back_recv.at[k],
            device_id={"dom": j}, device_id_type=MESH,
        )

    c_lo, c_hi, c_mid = slice(0, 2), slice(circ - 2, circ), slice(2, circ - 2)

    def shift(piece):
        return slice(piece.start + 2, piece.stop + 2)

    def halo(phase, pad, kind):
        if kind < 2:
            rows = (c_lo, c_hi)[kind]
            source = adj_ref.at[rows] if phase == 0 else pad.at[shift(rows), 2:radial + 2]
            target = pad.at[(slice(circ + 2, circ + 4), slice(0, 2))[kind], 2:radial + 2]
            device = {"sect": (left, right)[kind]}
        elif kind < 8:
            up = kind >= 5
            rows = (c_lo, c_hi, c_mid)[(kind - 2) % 3]
            first = radial - 2 if up else 0
            if phase == 0:
                source = adj_ref.at[rows, first:first + 2]
            else:
                source = pad.at[shift(rows), first + 2:first + 4]
            put = 0 if up else radial + 2
            target = pad.at[shift(rows), put:put + 2]
            device = {"dom": jnp.where(up, jnp.minimum(d + 1, dom_n - 1), jnp.maximum(d - 1, 0))}
        else:
            to_right = (kind - 8) % 2
            put = 0 if kind < 10 else radial + 2
            rows = (c_lo, c_hi)[to_right]
            source = pad.at[shift(rows), put:put + 2]
            target = pad.at[(slice(circ + 2, circ + 4), slice(0, 2))[to_right], put:put + 2]
            device = {"sect": (left, right)[to_right]}
        return pltpu.make_async_remote_copy(
            src_ref=source, dst_ref=target,
            send_sem=halo_send.at[phase, kind], recv_sem=halo_recv.at[phase, kind],
            device_id=device, device_id_type=MESH,
        )

    def start_dom(phase, pad, pieces):
        @pl.when(has_lo)
        def _():
            for kind in pieces:
                halo(phase, pad, 2 + kind).start()

        @pl.when(has_hi)
        def _():
            for kind in pieces:
                halo(phase, pad, 5 + kind).start()

    def forward_corners(phase, pad):
        @pl.when(has_lo)
        def _():
            for kind in (0, 1):
                halo(phase, pad, 5 + kind).wait_recv()
                halo(phase, pad, 8 + kind).start()

        @pl.when(has_hi)
        def _():
            for kind in (0, 1):
                halo(phase, pad, 2 + kind).wait_recv()
                halo(phase, pad, 10 + kind).start()

    def finish_halo(phase, pad):
        for kind in (0, 1):
            halo(phase, pad, kind).wait_recv()

        @pl.when(has_lo)
        def _():
            halo(phase, pad, 7).wait_recv()
            for kind in (8, 9):
                halo(phase, pad, kind).wait_recv()

        @pl.when(has_hi)
        def _():
            halo(phase, pad, 4).wait_recv()
            for kind in (10, 11):
                halo(phase, pad, kind).wait_recv()

    def drain_halo(phase, pad):
        for kind in (0, 1):
            halo(phase, pad, kind).wait_send()

        @pl.when(has_lo)
        def _():
            for kind in (2, 3, 4, 8, 9):
                halo(phase, pad, kind).wait_send()

        @pl.when(has_hi)
        def _():
            for kind in (5, 6, 7, 10, 11):
                halo(phase, pad, kind).wait_send()

    for k in range(1, dom_n):
        for copy in face_copies(k):
            copy.start()
    start_dom(0, pad0, (0, 1))
    for kind in (0, 1):
        halo(0, pad0, kind).start()
    start_dom(0, pad0, (2,))

    ids_recv[d] = ids_send[d]
    rows_recv[part(d), :] = rows_send[part(d), :]
    edge = jnp.zeros((circ + 4, 2, tile, cols), BF16)

    @pl.when(jnp.logical_not(has_lo))
    def _():
        pad0[:, 0:2] = edge
        pad1[:, 0:2] = edge

    @pl.when(jnp.logical_not(has_hi))
    def _():
        pad0[:, radial + 2:radial + 4] = edge
        pad1[:, radial + 2:radial + 4] = edge

    @pl.loop(0, circ * radial)
    def _(b):
        c = b // radial
        r = b % radial
        for k in range(codes):
            value = coupling_ref[c, r, k]
            q = value + (value >= 12).astype(jnp.int32)
            fifth = (q * 13) >> 6
            pick_c[b * codes + k] = c + jnp.clip(fifth, 0, 4)
            pick_r[b * codes + k] = r + jnp.clip(q - 5 * fifth, 0, 4)

    forward_corners(0, pad0)

    for k in range(1, dom_n):
        for copy in face_copies(k):
            copy.wait_recv()
    to_smem = pltpu.make_async_copy(ids_recv, ids_smem, local_sem.at[2])
    to_smem.start()
    groups = []
    share = 128 // per_peer
    for g in range(slots // 128):
        group = ids_recv[g * share][0:1]
        for q in range(1, share):
            group = group + ids_recv[g * share + q][0:1]
        groups.append(group)
    slot_nodes = jnp.concatenate(groups, axis=1)
    chunk = 256

    @pl.loop(0, circ * span // chunk)
    def _(t):
        local = lax.broadcasted_iota(jnp.int32, (chunk, slots), 0)
        hit = (local == slot_nodes - t * chunk).astype(F32).astype(BF16)
        load[pl.ds(pl.multiple_of(t * chunk, chunk), chunk), :] = jnp.dot(
            hit, rows_recv[...], preferred_element_type=F32
        )

    zeros = jnp.zeros((tile, cols), BF16)

    def relax(pad, blocks, store):
        rests = []
        for c, r in blocks:
            b = c * radial + r
            near = [pad[pick_c[b * codes + k], pick_r[b * codes + k]] for k in range(codes)]
            coupled = jnp.dot(
                tiles[c, r], jnp.concatenate([zeros] + near, axis=0),
                preferred_element_type=F32,
            )
            at = pl.ds(pl.multiple_of(b * tile, tile), tile)
            rests.append((load[at, :] - coupled).astype(BF16))
        for (c, r), rest in zip(blocks, rests):
            updated = jnp.dot(
                tiles[c, r, :, 0:2 * tile], jnp.concatenate([rest, zeros], axis=0),
                preferred_element_type=F32,
            ).astype(BF16)
            store(c, r, updated)

    def keep(c, r, value):
        pad1[c + 2, r + 2] = value

    def finish(c, r, value):
        result[c, r] = value
        at = pl.ds(pl.multiple_of((c * radial + r) * tile, tile), tile)
        final[at, :] = value.astype(F32)

    copy_adj.wait()
    copy_tiles.wait()
    finish_halo(0, pad0)
    group = 8
    per_row = radial // group

    @pl.loop(0, 4 * per_row)
    def _(t):
        row = t // per_row
        c = row + (row // 2) * (circ - 4)
        base = (t % per_row) * group
        relax(pad0, [(c, base + i) for i in range(group)], keep)

    start_dom(1, pad1, (0, 1))
    for kind in (0, 1):
        halo(1, pad1, kind).start()

    @pl.loop(2, circ - 2)
    def _(c):
        relax(pad0, [(c, r) for r in (0, 1, radial - 2, radial - 1)], keep)

    start_dom(1, pad1, (2,))

    @pl.loop(0, 2 * (circ - 4))
    def _(t):
        half = (radial - 4) // 2
        base = 2 + (t % 2) * half
        relax(pad0, [(2 + t // 2, base + i) for i in range(half)], keep)

    to_smem.wait()
    forward_corners(1, pad1)
    finish_halo(1, pad1)

    @pl.loop(0, circ * per_row)
    def _(t):
        c = t // per_row
        base = (t % per_row) * group
        relax(pad1, [(c, base + i) for i in range(group)], finish)

    write = pltpu.make_async_copy(result, adj_out, out_sem)
    write.start()

    def gather(j):
        offset = lax.rem(j * per_peer, 128)

        @pl.loop(0, per_peer // 16)
        def _(g):
            for i in range(16):
                p = g * 16 + i
                at = jnp.clip(ids_smem[j, 0, p + offset], 0, circ * span - 1)
                reply_f32[pl.ds(j * per_peer + p, 1), :] = final[pl.ds(at, 1), :]

    for k in range(1, dom_n):
        j = lax.rem(d + k, dom_n)
        gather(j)
        reply_send[part(j), :] = reply_f32[part(j), :].astype(BF16)
        back_copy(k).start()
    gather(d)
    reply_recv[part(d), :] = reply_f32[part(d), :].astype(BF16)

    drain_halo(0, pad0)
    drain_halo(1, pad1)
    for k in range(1, dom_n):
        for copy in face_copies(k):
            copy.wait_send()
    for k in range(1, dom_n):
        back_copy(k).wait()
    grad_out[0] = lax.dot_general(
        weight[...], reply_recv[...], (((0,), (0,)), ((), ())), preferred_element_type=F32
    ).astype(BF16)
    write.wait()


def solution(mesh):
    sect_n, dom_n = mesh.shape["sect"], mesh.shape["dom"]

    def shards(face_sens, face_owner, face_node, face_mask, adjoint_prev, block_rows, coupling):
        circ, radial, tile, cols = adjoint_prev.shape
        faces = face_sens.shape[1]
        per_peer = 2 * faces // dom_n
        slots = per_peer * dom_n
        nodes = circ * radial * tile
        pad = pltpu.VMEM((circ + 4, radial + 4, tile, cols), BF16)
        picks = pltpu.SMEM((circ * radial * coupling.shape[2],), jnp.int32)
        peer_sem = pltpu.SemaphoreType.DMA((dom_n,))
        vmem = pl.BlockSpec(memory_space=pltpu.VMEM)
        anywhere = pl.BlockSpec(memory_space=pl.ANY)
        return pl.pallas_call(
            functools.partial(kernel, sect_n, dom_n, per_peer),
            out_shape=(
                jax.ShapeDtypeStruct(adjoint_prev.shape, BF16),
                jax.ShapeDtypeStruct(face_sens.shape, BF16),
            ),
            in_specs=[vmem, vmem, vmem, vmem, pl.BlockSpec(memory_space=pltpu.SMEM), anywhere, anywhere],
            out_specs=(anywhere, vmem),
            scratch_shapes=[
                pad,
                pad,
                pltpu.VMEM(block_rows.shape, BF16),
                pltpu.VMEM((nodes, cols), F32),
                pltpu.VMEM((nodes, cols), F32),
                pltpu.VMEM(adjoint_prev.shape, BF16),
                pltpu.VMEM((slots, faces), BF16),
                pltpu.VMEM((slots, cols), BF16),
                pltpu.VMEM((slots, cols), BF16),
                pltpu.VMEM((dom_n, 8, 128), jnp.int32),
                pltpu.VMEM((dom_n, 8, 128), jnp.int32),
                pltpu.VMEM((slots, cols), F32),
                pltpu.VMEM((slots, cols), BF16),
                pltpu.VMEM((slots, cols), BF16),
                pltpu.SMEM((dom_n, 8, 128), jnp.int32),
                picks,
                picks,
                pltpu.SemaphoreType.DMA((2, 12)),
                pltpu.SemaphoreType.DMA((2, 12)),
                peer_sem, peer_sem, peer_sem, peer_sem, peer_sem, peer_sem,
                pltpu.SemaphoreType.DMA((3,)),
                pltpu.SemaphoreType.DMA,
            ],
            compiler_params=pltpu.CompilerParams(
                collective_id=0, has_side_effects=True, vmem_limit_bytes=48 * 1024 * 1024
            ),
        )(face_sens, face_owner, face_node, face_mask, coupling, adjoint_prev, block_rows)

    placed = (
        P("sect", "dom", None),
        P("sect", "dom"),
        P("sect", "dom"),
        P("sect", "dom"),
        P("sect", "dom", None, None),
        P("sect", "dom", None, None),
        P("sect", "dom", None),
    )
    return jax.shard_map(
        shards,
        mesh=mesh,
        in_specs=placed,
        out_specs=(P("sect", "dom", None, None), P("sect", "dom", None)),
        check_vma=False,
    )
```

time: 281 us -> 70.2 us (0.25); the launches traced: 278 us -> 69.9 us
  Pallas kernels: 0 us -> 61.9 us
  local copies, waits for them, and re-layouts: 59.1 us -> 7.36 us
  matrix products: 44.8 us -> 0 us
  blocking collectives: 44 us -> 0 us
  other arithmetic: 39.3 us -> 0 us
  waiting for transfers between devices: 37 us -> 0 us
  starting transfers between devices: 28.4 us -> 0 us
  between operations: 14.4 us -> 0.64 us
  loops' own time: 10.8 us -> 0 us
    pallas_call x0 -> x1, Pallas kernels: none -> 61.9 us  [shards(): pl.pallas_call(functools.partial(kernel, sect_n, dom_n, per_peer), out_sh...]
    dot_general x20 -> x0, matrix products: 44.8 us -> none  [the longest x2 20.8 us: shards(): jnp.einsum('cbij,cbjd->cbid', inverse, remainder, preferred_element_type=...]
    all_gather x2 -> x0, blocking collectives: 44 us -> none  [the longest x1 22 us: shards(): lax.all_gather(owner_ids, 'dom', axis=0, tiled=True)]
    gather x2 -> x0, local copies, waits for them, and re-layouts: 43.5 us -> none  [shards(): jnp.take(flat_blocks, pick_index, axis=0)]
    ppermute x8 -> x0, waiting for transfers between devices: 29.6 us -> none  [the longest x4 28.2 us: with_halo(): lax.ppermute(lax.slice_in_dim(block, block.shape[dim] - width, None, axis...]
    ppermute x8 -> x0, starting transfers between devices: 22.9 us -> none  [the longest x4 20.3 us: with_halo(): lax.ppermute(lax.slice_in_dim(block, block.shape[dim] - width, None, axis...]
    select_n x3 -> x0, other arithmetic: 21.5 us -> none  [shards(): jnp.take(flat_blocks, pick_index, axis=0)]
    another operation x2 -> x0, loops' own time: 10.8 us -> none  [the longest x1 5.49 us: pick_nodes(): total, unused = lax.scan(add_block, start, (circ_ids, flat_adjoint))]
  transfers between devices with their start and end apart: 10 -> 0, of which waited for: 5 -> 0; matrix products, arithmetic and copies ran while one was open for 17% -> 0% of each run, Pallas kernels for 0% -> 0%
where the time goes in v1:
time: 70.2 us; the launch traced here: 69.9 us
  Pallas kernels  61.9 us (88%)
  local copies, waits for them, and re-layouts  7.36 us (10%)
    pallas_call x1, Pallas kernels, shards(): pl.pallas_call(functools.partial(kernel, sect_n, dom_n, per_peer), out_sh...  61.9 us
    unnamed x13, local copies, waits for them, and re-layouts  7.36 us

profile of v1, /device:TPU:1, one launch (start us, length us, event | category | flops | bytes accessed | tf_op | source)
XLA Modules:
  0.0 69.9 jit_solution(14702766471301830263)
XLA Ops:
  0.6 0.8 %copy.9.coupling_ref = s32[8,16,5]{2,1,0:T(8,128)S(1)} copy(s32[8,16,5]{1,0,2:T(8,128)} %param.13) | data formatting | bytes 5120 | tf_op args[6]
  1.5 0.0 copy-start
  1.5 1.6 %copy-done = bf16[8,16,64,128]{3,2,1,0:T(8,128)(2,1)S(1)} copy-done((bf16[8,16,64,128]{3,2,1,0:T(8,128)(2,1)S(1)}, bf16[8,16,64,128]{3,2,1,0:T(8,128)(2,1)}, u32[]{:S(2)}) %copy-start) | copy-done | bytes 2097176
  3.1 0.0 copy-start.1
  3.1 0.9 %copy-done.1 = bf16[1,512,128]{2,1,0:T(8,128)(2,1)S(1)} copy-done((bf16[1,512,128]{2,1,0:T(8,128)(2,1)S(1)}, bf16[1,512,128]{2,1,0:T(8,128)(2,1)}, u32[]{:S(2)}) %copy-start.1) | copy-done | bytes 131096
  4.0 0.0 copy-start.2
  4.0 0.7 copy-done.2
  4.7 0.0 copy-start.3
  4.7 0.7 copy-done.3
  5.3 0.0 copy-start.4
  5.3 0.7 copy-done.4
  6.0 61.9 %shard_map.86 = (bf16[8,16,64,128]{3,2,1,0:T(8,128)(2,1)S(1)}, bf16[1,512,128]{2,1,0:T(8,128)(2,1)S(1)}) custom-call(bf16[1,512,128]{2,1,0:T(8,128)(2,1)S(1)} %copy-done.1, s32[1,512]{1,0:T(1,128)S(1)} %copy-done.2, s32[1,512]{1,0:T(1,128)S(1)} %copy-done.3, s32[1,512]{1,0:T(1,128)S(1)} %copy-done.4, s32[8,16,5]{2,1,0:T(8,128)S(1)} %copy.9.coupling_ref, ...), custom_call_target="tpu_custom_call" | custom-call | tf_op jit(solution)/shard_map/pallas_call | solution.py:374
  67.9 1.3 %copy.12 = bf16[8,16,64,128]{3,2,1,0:T(8,128)(2,1)} copy(bf16[8,16,64,128]{3,2,1,0:T(8,128)(2,1)S(1)} %get-tuple-element.4) | data formatting | bytes 4194304
  69.2 0.7 copy.13
Async XLA Ops:
  1.5 1.6 %copy-start = (bf16[8,16,64,128]{3,2,1,0:T(8,128)(2,1)S(1)}, bf16[8,16,64,128]{3,2,1,0:T(8,128)(2,1)}, u32[]{:S(2)}) copy-start(bf16[8,16,64,128]{3,2,1,0:T(8,128)(2,1)} %adj_ref.1) | copy-start | bytes 6291460
  3.1 0.9 %copy-start.1 = (bf16[1,512,128]{2,1,0:T(8,128)(2,1)S(1)}, bf16[1,512,128]{2,1,0:T(8,128)(2,1)}, u32[]{:S(2)}) copy-start(bf16[1,512,128]{2,1,0:T(8,128)(2,1)} %sens_ref.1) | copy-start | bytes 393220
  4.0 0.7 copy-start.2
  4.7 0.7 copy-start.3
  5.3 0.7 copy-start.4

commit v2 on v1

--- a/solution.py
+++ b/solution.py
@@ -14,8 +14,9 @@
 
 def kernel(
     sect_n, dom_n, per_peer,
-    sens_ref, owner_ref, node_ref, mask_ref, coupling_ref, adj_ref, block_ref,
+    sens_hbm, owner_hbm, node_hbm, mask_hbm, coupling_hbm, adj_ref, block_ref,
     adj_out, grad_out,
+    sens_ref, owner_ref, node_ref, mask_ref, coupling_ref, core0, core1,
     pad0, pad1, tiles, load, final, result, weight,
     rows_send, rows_recv, ids_send, ids_recv, reply_f32, reply_send, reply_recv,
     ids_smem, pick_c, pick_r,
@@ -23,7 +24,7 @@
     local_sem, out_sem,
 ):
     circ, radial, tile, cols = adj_ref.shape
-    codes = coupling_ref.shape[2]
+    codes = coupling_ref.shape[0]
     faces = sens_ref.shape[1]
     span = radial * tile
     slots = dom_n * per_peer
@@ -38,6 +39,19 @@
         adj_ref, pad0.at[2:circ + 2, 2:radial + 2], local_sem.at[0]
     )
     copy_tiles = pltpu.make_async_copy(block_ref, tiles, local_sem.at[1])
+    face_in = [
+        pltpu.make_async_copy(source, target, local_sem.at[3 + i])
+        for i, (source, target) in enumerate((
+            (owner_hbm, owner_ref), (mask_hbm, mask_ref), (node_hbm, node_ref),
+            (sens_hbm, sens_ref),
+        ))
+    ]
+    for copy in face_in:
+        copy.start()
+    copy_codes = pltpu.make_async_copy(coupling_hbm, coupling_ref, local_sem.at[7])
+    copy_codes.start()
+    copy_core = pltpu.make_async_copy(adj_ref, core0, local_sem.at[8])
+    copy_core.start()
     copy_adj.start()
     copy_tiles.start()
 
@@ -49,6 +63,8 @@
             barrier, inc=1, device_id={"dom": lax.rem(d + k, dom_n)}, device_id_type=MESH
         )
 
+    for copy in face_in:
+        copy.wait()
     owner = owner_ref[...]
     peers = max(dom_n, 8)
     hot = lax.broadcasted_iota(jnp.int32, (peers, faces), 0) == owner
@@ -220,12 +236,14 @@
         pad0[:, radial + 2:radial + 4] = edge
         pad1[:, radial + 2:radial + 4] = edge
 
+    copy_codes.wait()
+
     @pl.loop(0, circ * radial)
     def _(b):
         c = b // radial
         r = b % radial
         for k in range(codes):
-            value = coupling_ref[c, r, k]
+            value = coupling_ref[k, c, r]
             q = value + (value >= 12).astype(jnp.int32)
             fifth = (q * 13) >> 6
             pick_c[b * codes + k] = c + jnp.clip(fifth, 0, 4)
@@ -258,11 +276,14 @@
 
     zeros = jnp.zeros((tile, cols), BF16)
 
-    def relax(pad, blocks, store):
+    def relax(pad, blocks, store, less=0):
         rests = []
         for c, r in blocks:
             b = c * radial + r
-            near = [pad[pick_c[b * codes + k], pick_r[b * codes + k]] for k in range(codes)]
+            near = [
+                pad[pick_c[b * codes + k] - less, pick_r[b * codes + k] - less]
+                for k in range(codes)
+            ]
             coupled = jnp.dot(
                 tiles[c, r], jnp.concatenate([zeros] + near, axis=0),
                 preferred_element_type=F32,
@@ -278,50 +299,55 @@
 
     def keep(c, r, value):
         pad1[c + 2, r + 2] = value
+        core1[c, r] = value
 
     def finish(c, r, value):
         result[c, r] = value
         at = pl.ds(pl.multiple_of((c * radial + r) * tile, tile), tile)
         final[at, :] = value.astype(F32)
 
-    copy_adj.wait()
-    copy_tiles.wait()
-    finish_halo(0, pad0)
+    def inner_blocks(core, store):
+        half = (radial - 4) // 2
+
+        @pl.loop(0, 2 * (circ - 4))
+        def _(t):
+            base = 2 + (t % 2) * half
+            relax(core, [(2 + t // 2, base + i) for i in range(half)], store, 2)
+
     group = 8
     per_row = radial // group
 
-    @pl.loop(0, 4 * per_row)
-    def _(t):
-        row = t // per_row
-        c = row + (row // 2) * (circ - 4)
-        base = (t % per_row) * group
-        relax(pad0, [(c, base + i) for i in range(group)], keep)
-
+    def outer_rows(pad, store):
+        @pl.loop(0, 4 * per_row)
+        def _(t):
+            row = t // per_row
+            c = row + (row // 2) * (circ - 4)
+            base = (t % per_row) * group
+            relax(pad, [(c, base + i) for i in range(group)], store)
+
+    def outer_columns(pad, store):
+        @pl.loop(1, circ // 2 - 1)
+        def _(t):
+            ends = (0, 1, radial - 2, radial - 1)
+            relax(pad, [(2 * t + i, r) for i in range(2) for r in ends], store)
+
+    copy_core.wait()
+    copy_tiles.wait()
+    inner_blocks(core0, keep)
+    copy_adj.wait()
+    finish_halo(0, pad0)
+    outer_rows(pad0, keep)
     start_dom(1, pad1, (0, 1))
     for kind in (0, 1):
         halo(1, pad1, kind).start()
-
-    @pl.loop(2, circ - 2)
-    def _(c):
-        relax(pad0, [(c, r) for r in (0, 1, radial - 2, radial - 1)], keep)
-
+    outer_columns(pad0, keep)
     start_dom(1, pad1, (2,))
-
-    @pl.loop(0, 2 * (circ - 4))
-    def _(t):
-        half = (radial - 4) // 2
-        base = 2 + (t % 2) * half
-        relax(pad0, [(2 + t // 2, base + i) for i in range(half)], keep)
-
     to_smem.wait()
+    inner_blocks(core1, finish)
     forward_corners(1, pad1)
     finish_halo(1, pad1)
-
-    @pl.loop(0, circ * per_row)
-    def _(t):
-        c = t // per_row
-        base = (t % per_row) * group
-        relax(pad1, [(c, base + i) for i in range(group)], finish)
+    outer_rows(pad1, finish)
+    outer_columns(pad1, finish)
 
     write = pltpu.make_async_copy(result, adj_out, out_sem)
     write.start()
@@ -371,15 +397,23 @@
         peer_sem = pltpu.SemaphoreType.DMA((dom_n,))
         vmem = pl.BlockSpec(memory_space=pltpu.VMEM)
         anywhere = pl.BlockSpec(memory_space=pl.ANY)
+        codes = jnp.transpose(coupling, (2, 0, 1))
         return pl.pallas_call(
             functools.partial(kernel, sect_n, dom_n, per_peer),
             out_shape=(
                 jax.ShapeDtypeStruct(adjoint_prev.shape, BF16),
                 jax.ShapeDtypeStruct(face_sens.shape, BF16),
             ),
-            in_specs=[vmem, vmem, vmem, vmem, pl.BlockSpec(memory_space=pltpu.SMEM), anywhere, anywhere],
+            in_specs=[anywhere] * 7,
             out_specs=(anywhere, vmem),
             scratch_shapes=[
+                pltpu.VMEM(face_sens.shape, BF16),
+                pltpu.VMEM(face_owner.shape, jnp.int32),
+                pltpu.VMEM(face_owner.shape, jnp.int32),
+                pltpu.VMEM(face_owner.shape, jnp.int32),
+                pltpu.SMEM((coupling.shape[2], circ, radial), jnp.int32),
+                pltpu.VMEM(adjoint_prev.shape, BF16),
+                pltpu.VMEM(adjoint_prev.shape, BF16),
                 pad,
                 pad,
                 pltpu.VMEM(block_rows.shape, BF16),
@@ -400,13 +434,13 @@
                 pltpu.SemaphoreType.DMA((2, 12)),
                 pltpu.SemaphoreType.DMA((2, 12)),
                 peer_sem, peer_sem, peer_sem, peer_sem, peer_sem, peer_sem,
-                pltpu.SemaphoreType.DMA((3,)),
+                pltpu.SemaphoreType.DMA((9,)),
                 pltpu.SemaphoreType.DMA,
             ],
             compiler_params=pltpu.CompilerParams(
-                collective_id=0, has_side_effects=True, vmem_limit_bytes=48 * 1024 * 1024
+                collective_id=0, has_side_effects=True, vmem_limit_bytes=60 * 1024 * 1024
             ),
-        )(face_sens, face_owner, face_node, face_mask, coupling, adjoint_prev, block_rows)
+        )(face_sens, face_owner, face_node, face_mask, codes, adjoint_prev, block_rows)
 
     placed = (
         P("sect", "dom", None),

time: 70.2 us -> 66.1 us (0.942)
  local copies, waits for them, and re-layouts: 7.36 us -> 3.77 us
    unnamed x13 -> x4, local copies, waits for them, and re-layouts: 7.36 us -> 3.77 us
where the time goes in v2:
time: 66.1 us; the launch traced here: 65.9 us
  Pallas kernels  61.5 us (93%)
  local copies, waits for them, and re-layouts  3.77 us (6%)
    pallas_call x1, Pallas kernels, shards(): pl.pallas_call(functools.partial(kernel, sect_n, dom_n, per_peer), out_sh...  61.5 us
    unnamed x4, local copies, waits for them, and re-layouts  3.77 us

profile of v2, /device:TPU:1, one launch (start us, length us, event | category | flops | bytes accessed | tf_op | source)
XLA Modules:
  0.0 65.9 jit_solution(2630604361356188993)
XLA Ops:
  0.6 61.5 %shard_map.86 = (bf16[8,16,64,128]{3,2,1,0:T(8,128)(2,1)}, bf16[1,512,128]{2,1,0:T(8,128)(2,1)}) custom-call(bf16[1,512,128]{2,1,0:T(8,128)(2,1)} %sens_hbm.1, s32[1,512]{1,0:T(1,128)} %owner_hbm.1, s32[1,512]{1,0:T(1,128)} %node_hbm.1, s32[1,512]{1,0:T(1,128)} %mask_hbm.1, s32[5,8,16]{2,1,0:T(8,128)} %bitcast.1, bf16[8,16,64,128]{3,2,1,0:T(8,128)(2,1)} %adj_ref.1, ...), custom_call_target="tpu_custom_call" | custom-call | tf_op jit(solution)/shard_map/pallas_call | solution.py:401
  62.1 0.0 copy-start
  62.1 3.1 %copy.11 = bf16[8,16,64,128]{3,2,1,0:T(8,128)(2,1)} copy(bf16[8,16,64,128]{3,2,1,0:T(8,128)(2,1)} %get-tuple-element.4) | data formatting | bytes 4194304
  65.3 0.0 copy-done
  65.3 0.7 copy.12
Async XLA Ops:
  62.1 3.1 %copy-start = (bf16[1,512,128]{2,1,0:T(8,128)(2,1)S(1)}, bf16[1,512,128]{2,1,0:T(8,128)(2,1)}, u32[]{:S(2)}) copy-start(bf16[1,512,128]{2,1,0:T(8,128)(2,1)} %get-tuple-element.5) | copy-start | bytes 393220

commit v3 on v2

--- a/solution.py
+++ b/solution.py
@@ -10,6 +10,16 @@
 MESH = pl.DeviceIdType.MESH
 F32 = jnp.float32
 BF16 = jnp.bfloat16
+
+
+def partner(index, k):
+    other = index
+    bit = 1
+    while bit <= k:
+        if k & bit:
+            other = other + bit * (1 - 2 * ((index // bit) % 2))
+        bit *= 2
+    return other
 
 
 def kernel(
@@ -86,43 +96,44 @@
         weight[...], sens_ref[0], preferred_element_type=F32
     ).astype(BF16)
     across = (((1,), (1,)), ((), ()))
-    for j in range(dom_n):
+    for k in range(dom_n):
+        j = partner(d, k)
         if per_peer == 128:
-            chosen = weight[j * per_peer:(j + 1) * per_peer, :]
+            chosen = weight[pl.ds(pl.multiple_of(j * per_peer, per_peer), per_peer), :]
         else:
-            place = lax.broadcasted_iota(jnp.int32, (128, faces), 0)
-            place = place - lax.rem(d * per_peer, 128)
+            place = lax.broadcasted_iota(jnp.int32, (128, faces), 0) - k * per_peer % 128
             inside = (place >= 0) & (place < per_peer) & (place + j * per_peer == slot)
             chosen = inside.astype(F32).astype(BF16)
         high = lax.dot_general(node_hi, chosen, across, preferred_element_type=F32)
         low = lax.dot_general(node_lo, chosen, across, preferred_element_type=F32)
-        ids_send[j] = (high * 64.0 + low).astype(jnp.int32)
+        ids_send[k] = (high * 64.0 + low).astype(jnp.int32)
 
     pl.semaphore_wait(barrier, dom_n + 1)
 
     def part(start):
+        if isinstance(start, int):
+            return pl.ds(start * per_peer, per_peer)
         return pl.ds(pl.multiple_of(start * per_peer, per_peer), per_peer)
 
     def face_copies(k):
-        j = lax.rem(d + k, dom_n)
+        j = partner(d, k)
         ids = pltpu.make_async_remote_copy(
-            src_ref=ids_send.at[j], dst_ref=ids_recv.at[d],
+            src_ref=ids_send.at[k], dst_ref=ids_recv.at[k],
             send_sem=id_send.at[k], recv_sem=id_recv.at[k],
             device_id={"dom": j}, device_id_type=MESH,
         )
         rows = pltpu.make_async_remote_copy(
-            src_ref=rows_send.at[part(j)], dst_ref=rows_recv.at[part(d)],
+            src_ref=rows_send.at[part(j)], dst_ref=rows_recv.at[part(k)],
             send_sem=face_send.at[k], recv_sem=face_recv.at[k],
             device_id={"dom": j}, device_id_type=MESH,
         )
         return ids, rows
 
     def back_copy(k):
-        j = lax.rem(d + k, dom_n)
         return pltpu.make_async_remote_copy(
-            src_ref=reply_send.at[part(j)], dst_ref=reply_recv.at[part(d)],
+            src_ref=reply_send.at[part(k)], dst_ref=reply_recv.at[part(d)],
             send_sem=back_send.at[k], recv_sem=back_recv.at[k],
-            device_id={"dom": j}, device_id_type=MESH,
+            device_id={"dom": partner(d, k)}, device_id_type=MESH,
         )
 
     c_lo, c_hi, c_mid = slice(0, 2), slice(circ - 2, circ), slice(2, circ - 2)
@@ -214,7 +225,7 @@
             for kind in (5, 6, 7, 10, 11):
                 halo(phase, pad, kind).wait_send()
 
-    for k in range(1, dom_n):
+    for k in reversed(range(1, dom_n)):
         for copy in face_copies(k):
             copy.start()
     start_dom(0, pad0, (0, 1))
@@ -222,8 +233,8 @@
         halo(0, pad0, kind).start()
     start_dom(0, pad0, (2,))
 
-    ids_recv[d] = ids_send[d]
-    rows_recv[part(d), :] = rows_send[part(d), :]
+    ids_recv[0] = ids_send[0]
+    rows_recv[part(0), :] = rows_send[part(d), :]
     edge = jnp.zeros((circ + 4, 2, tile, cols), BF16)
 
     @pl.when(jnp.logical_not(has_lo))
@@ -249,30 +260,41 @@
             pick_c[b * codes + k] = c + jnp.clip(fifth, 0, 4)
             pick_r[b * codes + k] = r + jnp.clip(q - 5 * fifth, 0, 4)
 
+    chunk = 1024
+    half_n = dom_n // 2
+    wide = slots // 2
+
+    def face_sums(near):
+        base = 0 if near else half_n
+        for k in range(max(base, 1), base + half_n):
+            for copy in face_copies(k):
+                copy.wait_recv()
+        groups = []
+        share = 128 // per_peer
+        for g in range(wide // 128):
+            group = ids_recv[base + g * share][0:1]
+            for q in range(1, share):
+                group = group + ids_recv[base + g * share + q][0:1]
+            groups.append(group)
+        slot_nodes = jnp.concatenate(groups, axis=1)
+        local = lax.broadcasted_iota(jnp.int32, (chunk, wide), 0).astype(jnp.int32)
+
+        @pl.loop(0, circ * span // chunk)
+        def _(t):
+            offset = slot_nodes - t * chunk
+            hit = (local == offset).astype(F32).astype(BF16)
+            at = pl.ds(pl.multiple_of(t * chunk, chunk), chunk)
+            total = jnp.dot(
+                hit, rows_recv[base * per_peer:base * per_peer + wide, :],
+                preferred_element_type=F32,
+            )
+            load[at, :] = total if near else load[at, :] + total
+
+    face_sums(True)
     forward_corners(0, pad0)
-
-    for k in range(1, dom_n):
-        for copy in face_copies(k):
-            copy.wait_recv()
+    face_sums(False)
     to_smem = pltpu.make_async_copy(ids_recv, ids_smem, local_sem.at[2])
     to_smem.start()
-    groups = []
-    share = 128 // per_peer
-    for g in range(slots // 128):
-        group = ids_recv[g * share][0:1]
-        for q in range(1, share):
-            group = group + ids_recv[g * share + q][0:1]
-        groups.append(group)
-    slot_nodes = jnp.concatenate(groups, axis=1)
-    chunk = 256
-
-    @pl.loop(0, circ * span // chunk)
-    def _(t):
-        local = lax.broadcasted_iota(jnp.int32, (chunk, slots), 0)
-        hit = (local == slot_nodes - t * chunk).astype(F32).astype(BF16)
-        load[pl.ds(pl.multiple_of(t * chunk, chunk), chunk), :] = jnp.dot(
-            hit, rows_recv[...], preferred_element_type=F32
-        )
 
     zeros = jnp.zeros((tile, cols), BF16)
 
@@ -352,23 +374,22 @@
     write = pltpu.make_async_copy(result, adj_out, out_sem)
     write.start()
 
-    def gather(j):
-        offset = lax.rem(j * per_peer, 128)
+    def gather(k):
+        offset = k * per_peer % 128
 
         @pl.loop(0, per_peer // 16)
         def _(g):
             for i in range(16):
                 p = g * 16 + i
-                at = jnp.clip(ids_smem[j, 0, p + offset], 0, circ * span - 1)
-                reply_f32[pl.ds(j * per_peer + p, 1), :] = final[pl.ds(at, 1), :]
-
-    for k in range(1, dom_n):
-        j = lax.rem(d + k, dom_n)
-        gather(j)
-        reply_send[part(j), :] = reply_f32[part(j), :].astype(BF16)
+                at = jnp.clip(ids_smem[k, 0, p + offset], 0, circ * span - 1)
+                reply_f32[pl.ds(k * per_peer + p, 1), :] = final[pl.ds(at, 1), :]
+
+    for k in reversed(range(1, dom_n)):
+        gather(k)
+        reply_send[part(k), :] = reply_f32[part(k), :].astype(BF16)
         back_copy(k).start()
-    gather(d)
-    reply_recv[part(d), :] = reply_f32[part(d), :].astype(BF16)
+    gather(0)
+    reply_recv[part(d), :] = reply_f32[part(0), :].astype(BF16)
 
     drain_halo(0, pad0)
     drain_halo(1, pad1)

time: 66.1 us -> 60.4 us (0.914)
  Pallas kernels: 61.5 us -> 55.8 us
    pallas_call x1, Pallas kernels: 61.5 us -> 55.8 us  [shards(): pl.pallas_call(functools.partial(kernel, sect_n, dom_n, per_peer), out_sh...]
where the time goes in v3:
time: 60.4 us; the launch traced here: 60.3 us
  Pallas kernels  55.8 us (92%)
  local copies, waits for them, and re-layouts  3.77 us (6%)
  between operations  0.65 us (1%)
    pallas_call x1, Pallas kernels, shards(): pl.pallas_call(functools.partial(kernel, sect_n, dom_n, per_peer), out_sh...  55.8 us
    unnamed x4, local copies, waits for them, and re-layouts  3.77 us

profile of v3, /device:TPU:1, one launch (start us, length us, event | category | flops | bytes accessed | tf_op | source)
XLA Modules:
  0.0 60.3 jit_solution(4071883224343348769)
XLA Ops:
  0.6 55.8 %shard_map.86 = (bf16[8,16,64,128]{3,2,1,0:T(8,128)(2,1)}, bf16[1,512,128]{2,1,0:T(8,128)(2,1)}) custom-call(bf16[1,512,128]{2,1,0:T(8,128)(2,1)} %sens_hbm.1, s32[1,512]{1,0:T(1,128)} %owner_hbm.1, s32[1,512]{1,0:T(1,128)} %node_hbm.1, s32[1,512]{1,0:T(1,128)} %mask_hbm.1, s32[5,8,16]{2,1,0:T(8,128)} %bitcast.1, bf16[8,16,64,128]{3,2,1,0:T(8,128)(2,1)} %adj_ref.1, ...), custom_call_target="tpu_custom_call" | custom-call | tf_op jit(solution)/shard_map/pallas_call | solution.py:422
  56.5 0.0 copy-start
  56.5 3.1 %copy.11 = bf16[8,16,64,128]{3,2,1,0:T(8,128)(2,1)} copy(bf16[8,16,64,128]{3,2,1,0:T(8,128)(2,1)} %get-tuple-element.4) | data formatting | bytes 4194304
  59.6 0.0 copy-done
  59.6 0.7 %copy.12 = bf16[1,512,128]{2,1,0:T(8,128)(2,1)} copy(bf16[1,512,128]{2,1,0:T(8,128)(2,1)S(1)} %copy-done) | data formatting | bytes 262144
Async XLA Ops:
  56.5 3.1 %copy-start = (bf16[1,512,128]{2,1,0:T(8,128)(2,1)S(1)}, bf16[1,512,128]{2,1,0:T(8,128)(2,1)}, u32[]{:S(2)}) copy-start(bf16[1,512,128]{2,1,0:T(8,128)(2,1)} %get-tuple-element.5) | copy-start | bytes 393220
